TPU v7x, 32 devices: a whole 2x2x4 slice. The times are simulated.
32 devices in a mesh: batch: 8 (over z, y), blk: 4 (over x, core).
Axes of the slice: x: 2, y: 2, z: 4, core: 2. Of those that a mesh axis runs over, the one named last changes fastest.
Arguments:
- tokens: bfloat16 [8192, 768], P(('batch', 'blk')), may hold values from -6 to 6
- memory: bfloat16 [8, 512, 768], P('batch', 'blk'), may hold values from -6 to 6
- mem_pos: int32 [8, 512], P('batch', 'blk'), may hold values from 0 to 4095
- seg_count: int32 [8], P('batch'), may hold values from 1 to 4, as said below
- w_qkv: bfloat16 [2, 768, 2304], replicated, may hold values from -0.21875 to 0.21875
- w_out: bfloat16 [2, 768, 768], replicated, may hold values from -0.875 to 0.875
- w_up: bfloat16 [2, 768, 3072], replicated, may hold values from -0.21875 to 0.21875
- w_down: bfloat16 [2, 3072, 768], replicated, may hold values from -0.109375 to 0.109375
- gain_attn: float32 [2, 768], replicated, may hold values from 0.5 to 1.5
- gain_mlp: float32 [2, 768], replicated, may hold values from 0.5 to 1.5
- w_mu: float32 [2, 256], replicated, may hold values from -0.1875 to 0.1875
- w_sig: float32 [2, 256], replicated, may hold values from -0.1875 to 0.1875
- cotangent: bfloat16 [8192, 768], P(('batch', 'blk')), may hold values from -6 to 6
Outputs:
- mixed: bfloat16 [8192, 768], P(('batch', 'blk'))
- d_tokens: float32 [8192, 768], P(('batch', 'blk'))
- d_w_qkv: float32 [2, 768, 2304], P(None, 'blk')
- d_w_out: float32 [2, 768, 768], P(None, 'blk')
- d_w_up: float32 [2, 768, 3072], P(None, 'blk')
- d_w_down: float32 [2, 3072, 768], P(None, 'blk')
- d_gain_attn: float32 [2, 768], P(None, 'blk')
- d_gain_mlp: float32 [2, 768], P(None, 'blk')
- d_w_mu: float32 [2, 256], P(None, 'blk')
- d_w_sig: float32 [2, 256], P(None, 'blk')
Inputs may be any that keep to these rules, and one draw needn't show every extreme that they name: `seg_count`: some document fills all 4 segments; most are short.
All inputs are finite; a program needn't handle non-finite values.
Results may differ from a plain program's by a relative error of at most 0.018.
Values may be sent and summed in bfloat16 or wider, within the bound.
No kernel may reach another device: no remote copies, remote signals or barrier semaphores. Data moves between devices by JAX's collectives and lax.ppermute only.
A program may use at most 448 MiB of HBM per device.

v0:
```python
import jax
import jax.numpy as jnp
from jax import lax
from jax.sharding import PartitionSpec as P

HEADS = 12
HEAD = 64
D = 768
NBASIS = 256
LAYERS = 2
MEMPOS = 4096


highest = lax.Precision.HIGHEST
ridge_weight = 0.5


def layer_norm(inputs, gain):
    average = jnp.mean(inputs, axis=-1, keepdims=True)
    centred = inputs - average
    spread = jnp.mean(centred * centred, axis=-1, keepdims=True)
    return centred * lax.rsqrt(spread + 1e-05) * gain


def centres_of(count):
    return (jnp.arange(count).astype(jnp.float32) + 0.5) / count


def density(scores, weight_mu, weight_sig):
    count = scores.shape[-1]
    breadth = 1.0 / count
    place = jax.nn.sigmoid(jnp.sum(scores * weight_mu, axis=-1, keepdims=True))
    variance = (0.5 + jax.nn.softplus(jnp.sum(scores * weight_sig, axis=-1, keepdims=True))) / 64.0
    offset = place - centres_of(count)
    return jnp.sqrt(breadth * breadth / variance) * jnp.exp(-offset * offset / (2.0 * variance))


def basis_table(positions):
    breadth = 1.0 / NBASIS
    times = (positions.astype(jnp.float32) + 0.5) / MEMPOS
    offset = times[:, None] - centres_of(NBASIS)[None, :]
    return jnp.exp(-offset * offset / (2.0 * breadth * breadth))


def gelu_piece(upward):
    return jax.nn.gelu(upward, approximate=True)


def masked_scores(query, keys, allowed, scale):
    scores = jnp.einsum("qhd,khd->hqk", query, keys, preferred_element_type=jnp.float32) * scale
    return jnp.where(allowed[None], scores, -1e30)


def on_device(
    tokens,
    memory,
    mem_pos,
    seg_count,
    w_qkv,
    w_out,
    w_up,
    w_down,
    gain_attn,
    gain_mlp,
    w_mu,
    w_sig,
    cotangent,
):
    rows = tokens.shape[0]
    width = D
    heads = HEADS
    head = HEAD
    seq = rows * lax.axis_size("blk")
    scale = HEAD ** (-0.5)
    length = seg_count[0] * rows
    first = lax.axis_index("blk") * rows
    own_places = first + jnp.arange(rows, dtype=jnp.int32)
    all_places = jnp.arange(seq, dtype=jnp.int32)
    allowed = (all_places[None, :] <= own_places[:, None]) & (all_places[None, :] < length)
    basis = basis_table(mem_pos[0])
    samples = memory[0].astype(jnp.float32)
    gram, right = lax.psum(
        (jnp.dot(basis.T, basis, precision=highest), jnp.dot(basis.T, samples, precision=highest)),
        "blk",
    )
    gram = gram + ridge_weight * jnp.eye(NBASIS, dtype=jnp.float32)
    factor = jnp.linalg.cholesky(gram)
    coeff_low = jax.scipy.linalg.cho_solve((factor, True), right).astype(jnp.bfloat16)
    coeff_wide = coeff_low.astype(jnp.float32)
    hidden = tokens.astype(jnp.float32)
    saved = []
    for layer in range(LAYERS):
        normed = layer_norm(hidden, gain_attn[layer]).astype(jnp.bfloat16)
        qkv = jnp.dot(normed, w_qkv[layer], preferred_element_type=jnp.float32).astype(jnp.bfloat16)
        query = qkv[:, :width].reshape(rows, heads, head)
        kv_whole = lax.all_gather(qkv[:, width:], "blk", axis=0, tiled=True)
        keys = kv_whole[:, :width].reshape(seq, heads, head)
        values = kv_whole[:, width:].reshape(seq, heads, head)
        scores = masked_scores(query, keys, allowed, scale)
        peak = jnp.max(scores, axis=-1, keepdims=True)
        expo = jnp.exp(scores - peak)
        total = jnp.sum(expo, axis=-1, keepdims=True)
        probs = (expo / total).astype(jnp.bfloat16)
        log_total = peak + jnp.log(total)
        local = jnp.einsum("hqk,khd->qhd", probs, values, preferred_element_type=jnp.float32)
        memory_kv = jnp.dot(
            coeff_low, w_qkv[layer][:, width:], preferred_element_type=jnp.float32
        ).astype(jnp.bfloat16)
        mem_keys = memory_kv[:, :width].reshape(NBASIS, heads, head)
        mem_values = memory_kv[:, width:].reshape(NBASIS, heads, head)
        mem_scores = (
            jnp.einsum("qhd,nhd->hqn", query, mem_keys, preferred_element_type=jnp.float32) * scale
        )
        weights = density(mem_scores, w_mu[layer], w_sig[layer]).astype(jnp.bfloat16)
        recalled = jnp.einsum(
            "hqn,nhd->qhd", weights, mem_values, preferred_element_type=jnp.float32
        )
        attended = (local + recalled).reshape(rows, width).astype(jnp.bfloat16)
        middle = hidden + jnp.dot(attended, w_out[layer], preferred_element_type=jnp.float32)
        normed2 = layer_norm(middle, gain_mlp[layer]).astype(jnp.bfloat16)
        upward = jnp.dot(normed2, w_up[layer], preferred_element_type=jnp.float32)
        active = gelu_piece(upward).astype(jnp.bfloat16)
        kv_kept = kv_whole
        saved.append(
            (
                hidden,
                normed,
                qkv,
                kv_kept,
                log_total,
                memory_kv,
                attended,
                middle,
                normed2,
                upward,
                active,
            )
        )
        hidden = middle + jnp.dot(active, w_down[layer], preferred_element_type=jnp.float32)
    live = (own_places < length).astype(jnp.float32)[:, None]
    grad = cotangent.astype(jnp.float32) * live
    grads_qkv, grads_out, grads_up, grads_down = ([], [], [], [])
    grads_gain_attn, grads_gain_mlp, grads_mu, grads_sig = ([], [], [], [])
    for layer in reversed(range(LAYERS)):
        (
            layer_input,
            normed,
            qkv,
            kv_kept,
            log_total,
            memory_kv,
            attended,
            middle,
            normed2,
            upward,
            active,
        ) = saved[layer]
        grad_low = grad.astype(jnp.bfloat16)
        d_down = jnp.dot(active.T, grad_low, preferred_element_type=jnp.float32)
        d_active = jnp.dot(grad_low, w_down[layer].T, preferred_element_type=jnp.float32)
        unused, gelu_back = jax.vjp(gelu_piece, upward)
        d_upward = gelu_back(d_active)[0].astype(jnp.bfloat16)
        d_up = jnp.dot(normed2.T, d_upward, preferred_element_type=jnp.float32)
        d_normed2 = jnp.dot(d_upward, w_up[layer].T, preferred_element_type=jnp.float32)
        unused, norm_back = jax.vjp(layer_norm, middle, gain_mlp[layer])
        d_middle, d_gain_mlp = norm_back(d_normed2)
        grad = grad + d_middle
        grad_low = grad.astype(jnp.bfloat16)
        d_out = jnp.dot(attended.T, grad_low, preferred_element_type=jnp.float32)
        d_attended = jnp.dot(grad_low, w_out[layer].T, preferred_element_type=jnp.float32).astype(
            jnp.bfloat16
        )
        d_heads = d_attended.reshape(rows, heads, head)
        kv_whole = kv_kept
        query = qkv[:, :width].reshape(rows, heads, head)
        keys = kv_whole[:, :width].reshape(seq, heads, head)
        values = kv_whole[:, width:].reshape(seq, heads, head)
        scores = masked_scores(query, keys, allowed, scale)
        probs = jnp.exp(scores - log_total)
        probs_low = probs.astype(jnp.bfloat16)
        d_probs = jnp.einsum("qhd,khd->hqk", d_heads, values, preferred_element_type=jnp.float32)
        correction = jnp.sum(probs * d_probs, axis=-1, keepdims=True)
        d_scores = (probs * (d_probs - correction)).astype(jnp.bfloat16)
        d_query = (
            jnp.einsum("hqk,khd->qhd", d_scores, keys, preferred_element_type=jnp.float32) * scale
        )
        d_keys = (
            jnp.einsum("hqk,qhd->khd", d_scores, query, preferred_element_type=jnp.float32) * scale
        )
        d_values = jnp.einsum(
            "hqk,qhd->khd", probs_low, d_heads, preferred_element_type=jnp.float32
        )
        whole_terms = jnp.concatenate([d_keys.reshape(seq, width), d_values.reshape(seq, width)], 1)
        d_kv = lax.psum_scatter(whole_terms, "blk", scatter_dimension=0, tiled=True)
        mem_keys = memory_kv[:, :width].reshape(NBASIS, heads, head)
        mem_values = memory_kv[:, width:].reshape(NBASIS, heads, head)
        mem_scores = (
            jnp.einsum("qhd,nhd->hqn", query, mem_keys, preferred_element_type=jnp.float32) * scale
        )
        weights, density_back = jax.vjp(density, mem_scores, w_mu[layer], w_sig[layer])
        weights_low = weights.astype(jnp.bfloat16)
        d_weights = jnp.einsum(
            "qhd,nhd->hqn", d_heads, mem_values, preferred_element_type=jnp.float32
        )
        d_mem_values = jnp.einsum(
            "hqn,qhd->nhd", weights_low, d_heads, preferred_element_type=jnp.float32
        )
        d_mem_scores, d_mu, d_sig = density_back(d_weights)
        d_mem_low = d_mem_scores.astype(jnp.bfloat16)
        d_query = (
            d_query
            + jnp.einsum("hqn,nhd->qhd", d_mem_low, mem_keys, preferred_element_type=jnp.float32)
            * scale
        )
        d_mem_keys = (
            jnp.einsum("hqn,qhd->nhd", d_mem_low, query, preferred_element_type=jnp.float32) * scale
        )
        d_memory_kv = jnp.concatenate(
            [d_mem_keys.reshape(NBASIS, width), d_mem_values.reshape(NBASIS, width)], 1
        )
        d_qkv = jnp.concatenate([d_query.reshape(rows, width), d_kv], 1).astype(jnp.bfloat16)
        token_part = jnp.dot(normed.T, d_qkv, preferred_element_type=jnp.float32)
        memory_part = jnp.dot(coeff_wide.T, d_memory_kv, precision=highest)
        d_qkv_weight = jnp.concatenate(
            [token_part[:, :width], token_part[:, width:] + memory_part], 1
        )
        d_normed = jnp.dot(d_qkv, w_qkv[layer].T, preferred_element_type=jnp.float32)
        unused, norm_back = jax.vjp(layer_norm, layer_input, gain_attn[layer])
        d_input, d_gain_attn = norm_back(d_normed)
        grad = grad + d_input
        grads_qkv.insert(0, d_qkv_weight)
        grads_out.insert(0, d_out)
        grads_up.insert(0, d_up)
        grads_down.insert(0, d_down)
        grads_gain_attn.insert(0, d_gain_attn)
        grads_gain_mlp.insert(0, d_gain_mlp)
        grads_mu.insert(0, d_mu)
        grads_sig.insert(0, d_sig)
    shares = (
        lax.psum_scatter(jnp.stack(grads_qkv), "blk", scatter_dimension=1, tiled=True),
        lax.psum_scatter(jnp.stack(grads_out), "blk", scatter_dimension=1, tiled=True),
        lax.psum_scatter(jnp.stack(grads_up), "blk", scatter_dimension=1, tiled=True),
        lax.psum_scatter(jnp.stack(grads_down), "blk", scatter_dimension=1, tiled=True),
        lax.psum_scatter(jnp.stack(grads_gain_attn), "blk", scatter_dimension=1, tiled=True),
        lax.psum_scatter(jnp.stack(grads_gain_mlp), "blk", scatter_dimension=1, tiled=True),
        lax.psum_scatter(jnp.stack(grads_mu), "blk", scatter_dimension=1, tiled=True),
        lax.psum_scatter(jnp.stack(grads_sig), "blk", scatter_dimension=1, tiled=True),
    )
    totals = lax.psum(
        (shares[0], shares[1], shares[2], shares[3], shares[4], shares[5], shares[6], shares[7]),
        "batch",
    )
    return (
        hidden.astype(jnp.bfloat16),
        grad,
        totals[0],
        totals[1],
        totals[2],
        totals[3],
        totals[4],
        totals[5],
        totals[6],
        totals[7],
    )


def solution(mesh):
    placed = (
        P(("batch", "blk"), None),
        P("batch", "blk", None),
        P("batch", "blk"),
        P("batch"),
        P(),
        P(),
        P(),
        P(),
        P(),
        P(),
        P(),
        P(),
        P(("batch", "blk"), None),
    )
    return jax.shard_map(
        on_device,
        mesh=mesh,
        in_specs=placed,
        out_specs=(
            P(("batch", "blk"), None),
            P(("batch", "blk"), None),
            P(None, "blk", None),
            P(None, "blk", None),
            P(None, "blk", None),
            P(None, "blk", None),
            P(None, "blk"),
            P(None, "blk"),
            P(None, "blk"),
            P(None, "blk"),
        ),
        check_vma=False,
    )
```

profile of v0, /device:TPU:0, one launch (start us, length us, event | category | flops | bytes accessed | tf_op | source)
XLA Modules:
  0.0 1427.0 jit_solution(9331867180450010863)
XLA Ops:
  14.5 3.3 convolution_convert_fusion.1
  19.2 6.5 slice_bitcast_fusion
  27.0 23.0 %all-reduce.9.cloned.1.call-done = (f32[256,768]{1,0:T(8,128)}, f32[256,256]{1,0:T(8,128)}) async-done(((f32[256,768]{1,0:T(8,128)}, f32[256,256]{1,0:T(8,128)}), (f32[256,768]{1,0:T(8,128)}, f32[256,256]{1,0:T(8,128)})) %all-reduce.9.cloned.1.call-update) | async-done | bytes 1048592 | tf_op jit(solution)/shard_map/psum | solution.py:82
  52.2 11.7 cholesky.49
  63.9 9.8 custom-call.18
  74.2 11.7 cholesky.103
  88.0 4.5 while.1
  92.5 19.7 %custom-call.19 = f32[2,128,128]{1,2,0:T(8,128)S(1)} custom-call(f32[2,128,128]{2,1,0:T(8,128)S(1)} %get-tuple-element.25), custom_call_target="InvertDiagBlocksLowerTriangular" | custom-call | tf_op jit(solution)/shard_map/jit(_cho_solve)/triangular_solve | solution.py:88
  116.5 2.3 multiply_reduce_fusion.10
  118.9 3.8 fusion.273
  124.5 3.1 copy.77
  127.6 2.3 fusion.28
  130.0 3.8 fusion
  133.8 2.4 copy-done.2
  136.2 3.6 fusion.10
  150.7 2.4 convolution_convert_fusion.2
  154.9 2.3 multiply_reduce_fusion.8
  157.3 22.3 %all-gather.5.cloned.1.call-done = bf16[1024,1536]{1,0:T(8,128)(2,1)} async-done(((bf16[256,1536]{1,0:T(8,128)(2,1)}), bf16[1024,1536]{1,0:T(8,128)(2,1)}) %all-gather.5.cloned.1.call-update) | async-done | bytes 3145744 | tf_op jit(solution)/shard_map/all_gather | solution.py:96
  179.6 3.7 fusion.272
  185.4 6.8 fusion.29
  192.1 2.6 copy.84
  194.7 8.3 fusion.1
  203.0 5.3 fusion.11
  212.6 6.2 fusion.73
  218.9 2.2 multiply_reduce_fusion.12
  226.5 10.9 multiply_reduce_fusion.1
  237.4 7.6 fusion.6
  245.1 7.0 multiply_convert_fusion.1
  254.7 3.4 pad_maximum_fusion.3
  259.1 4.0 fusion.54
  267.5 49.1 %reduce-scatter.19.cloned.1.call-done = f32[256,1536]{0,1:T(8,128)} async-done(((f32[1024,1536]{0,1:T(8,128)}), f32[256,1536]{0,1:T(8,128)}) %reduce-scatter.19.cloned.1.call-update) | async-done | bytes 1572880 | tf_op jit(solution)/shard_map/reduce_scatter | solution.py:194
  318.2 4.4 multiply_reduce_fusion.14
  324.5 5.7 fusion.66
  335.0 11.2 multiply_reduce_fusion
  346.1 7.6 fusion.4
  353.8 6.8 multiply_convert_fusion
  363.3 3.4 pad_maximum_fusion.4
  368.9 2.5 pad_maximum_fusion.5
  371.5 5.2 convolution_bitcast_fusion
  378.9 7.0 pad_maximum_fusion.1
  386.1 3.1 convolution_bitcast_fusion.2
  390.8 7.0 pad_maximum_fusion
  404.1 2.9 fusion.57
  409.3 2.9 slice_add_fusion
  416.3 3.4 maximum_bitcast_fusion.1
  419.7 5.6 reduce-scatter.21.cloned.1.call-done
  428.3 2.9 slice_add_fusion.1
  431.2 3.6 maximum_bitcast_fusion
  434.8 13.1 pad_maximum_fusion.2
  448.7 2.7 multiply_reduce_fusion.2
  455.3 3.7 fusion.171
  460.5 15.7 %reduce-scatter.25.cloned.1.call-done = f32[2,192,768]{2,1,0:T(8,128)} async-done(((f32[2,768,768]{2,1,0:T(8,128)}), f32[2,192,768]{2,1,0:T(8,128)}) %reduce-scatter.25.cloned.1.call-update) | async-done | bytes 1179664 | tf_op jit(solution)/shard_map/reduce_scatter | solution.py:241
  476.3 142.1 %reduce-scatter.29.cloned.1.call-done = f32[2,768,768]{2,1,0:T(8,128)} async-done(((f32[2,3072,768]{2,1,0:T(8,128)}), f32[2,768,768]{2,1,0:T(8,128)}) %reduce-scatter.29.cloned.1.call-update) | async-done | bytes 4718608 | tf_op jit(solution)/shard_map/reduce_scatter | solution.py:243
  618.4 142.3 %reduce-scatter.27.cloned.1.call-done = f32[2,192,3072]{2,1,0:T(8,128)} async-done(((f32[2,768,3072]{2,1,0:T(8,128)}), f32[2,192,3072]{2,1,0:T(8,128)}) %reduce-scatter.27.cloned.1.call-update) | async-done | bytes 4718608 | tf_op jit(solution)/shard_map/reduce_scatter | solution.py:242
  760.6 112.1 %reduce-scatter.23.cloned.1.call-done = f32[2,192,2304]{2,1,0:T(8,128)} async-done(((f32[2,768,2304]{2,1,0:T(8,128)}), f32[2,192,2304]{2,1,0:T(8,128)}) %reduce-scatter.23.cloned.1.call-update) | async-done | bytes 3538960 | tf_op jit(solution)/shard_map/reduce_scatter | solution.py:240
  873.9 6.0 fusion.142
  879.9 14.7 %reduce-scatter.37.cloned.1.call-done = f32[64,2]{1,0:T(8,128)} async-done(((f32[256,2]{1,0:T(8,128)}), f32[64,2]{1,0:T(8,128)}) %reduce-scatter.37.cloned.1.call-update) | async-done | bytes 528
  895.5 21.3 %reduce-scatter.35.cloned.1.call-done = f32[64,2]{1,0:T(8,128)} async-done(((f32[256,2]{1,0:T(8,128)}), f32[64,2]{1,0:T(8,128)}) %reduce-scatter.35.cloned.1.call-update) | async-done | bytes 528
  917.6 22.9 %reduce-scatter.33.cloned.1.call-done = f32[192,2]{1,0:T(8,128)} async-done(((f32[768,2]{1,0:T(8,128)}), f32[192,2]{1,0:T(8,128)}) %reduce-scatter.33.cloned.1.call-update) | async-done | bytes 1552
  942.7 21.8 %reduce-scatter.31.cloned.1.call-done = f32[192,2]{1,0:T(8,128)} async-done(((f32[768,2]{1,0:T(8,128)}), f32[192,2]{1,0:T(8,128)}) %reduce-scatter.31.cloned.1.call-update) | async-done | bytes 1552
  965.4 22.7 %all-reduce.1 = (f32[2,192]{1,0:T(2,128)}, f32[2,192]{1,0:T(2,128)}, f32[2,64]{1,0:T(2,128)}, f32[2,64]{1,0:T(2,128)}) all-reduce(f32[2,192]{1,0:T(2,128)S(1)} %copy.99, f32[2,192]{1,0:T(2,128)S(1)} %copy.101, f32[2,64]{1,0:T(2,128)S(1)} %copy.103, f32[2,64]{1,0:T(2,128)S(1)} %copy.105), channel_id=1, replica_groups=mesh['batch'=8,'blk'=4] {'batch'}, use_global_device_ids=true, to_apply=%region_51.53 | all-reduce | flops 1024 | bytes 8192 | tf_op jit(solution)/shard_map/psum | solution.py:249
  988.2 421.2 %all-reduce.7.cloned.1.call-done = (f32[2,192,2304]{2,1,0:T(8,128)}, f32[2,192,768]{2,1,0:T(8,128)}, f32[2,192,3072]{2,1,0:T(8,128)}, f32[2,768,768]{2,1,0:T(8,128)}) async-done(((f32[2,192,2304]{2,1,0:T(8,128)}, f32[2,192,768]{2,1,0:T(8,128)}, f32[2,192,3072]{2,1,0:T(8,128)}, f32[2,768,768]{2,1,0:T(8,128)}), (f32[2,192,2304]{2,1,0:T(8,128)}, f32[2,192,768]{2,1,0:T(8,128)}, f32[2,192,3072]{2,1,0:T(8,128)}, ...) | async-done | bytes 14155792 | tf_op jit(solution)/shard_map/psum | solution.py:249
  1409.4 4.2 copy.124
  1414.6 2.4 copy.126
  (442 shorter events, 102.6 us)
Async XLA Ops:
  7.2 42.8 %all-reduce.9.cloned.1.call-start = ((), (), s32[]{:S(2)}) async-start(), calls=%async_computation.23 | async-start | bytes 2097152 | tf_op jit(solution)/shard_map/psum | solution.py:82
  10.7 108.3 %all-gather.3.cloned.1.call-start = ((), (), s32[]{:S(2)}) async-start(), calls=%async_computation.10 | async-start | bytes 3932160 | tf_op jit(solution)/shard_map/all_gather | solution.py:96
  11.8 6.0 copy-start.82
  18.8 160.8 %all-gather.5.cloned.1.call-start = ((), (), s32[]{:S(2)}) async-start(), calls=%async_computation.11 | async-start | bytes 3932160 | tf_op jit(solution)/shard_map/all_gather | solution.py:96
  19.1 6.8 copy-start.97
  19.2 6.8 copy-start.98
  19.2 7.5 copy-start.90
  25.9 101.7 %copy-start.20 = (bf16[256,768]{0,1:T(8,128)(2,1)}, bf16[256,768]{0,1:T(8,128)(2,1)S(1)}, u32[]{:S(2)}) copy-start(bf16[256,768]{0,1:T(8,128)(2,1)S(1)} %copy.78) | copy-start | bytes 1179652
  25.9 26.2 %copy-start.93 = (f32[1,256]{1,0:T(1,128)}, f32[1,256]{1,0:T(1,128)S(1)}, u32[]{:S(2)}) copy-start(f32[1,256]{1,0:T(1,128)S(1)} %get-tuple-element.111) | copy-start | bytes 3076
  26.0 26.2 %copy-start.95 = (f32[1,256]{1,0:T(1,128)}, f32[1,256]{1,0:T(1,128)S(1)}, u32[]{:S(2)}) copy-start(f32[1,256]{1,0:T(1,128)S(1)} %get-tuple-element.113) | copy-start | bytes 3076
  49.9 62.3 %copy-start.68 = (f32[256,768]{1,0:T(8,128)S(1)}, f32[256,768]{1,0:T(8,128)}, u32[]{:S(2)}) copy-start(f32[256,768]{1,0:T(8,128)} %get-tuple-element.68) | copy-start | bytes 2359300
  114.3 36.3 %copy-start.45 = (bf16[128,768]{1,0:T(8,128)(2,1)}, bf16[128,768]{1,0:T(8,128)(2,1)S(1)}, u32[]{:S(2)}) copy-start(bf16[128,768]{1,0:T(8,128)(2,1)S(1)} %get-tuple-element.118) | copy-start | bytes 589828
  115.3 35.3 %copy-start.47 = (bf16[128,768]{1,0:T(8,128)(2,1)}, bf16[128,768]{1,0:T(8,128)(2,1)S(1)}, u32[]{:S(2)}) copy-start(bf16[128,768]{1,0:T(8,128)(2,1)S(1)} %convolution_convert_fusion.6) | copy-start | bytes 589828
  116.3 6.4 copy-start.52
  116.5 23.3 %copy-start.71 = (bf16[256,768]{0,1:T(8,128)(2,1)}, bf16[256,768]{0,1:T(8,128)(2,1)S(1)}, u32[]{:S(2)}) copy-start(bf16[256,768]{0,1:T(8,128)(2,1)S(1)} %copy.81) | copy-start | bytes 1179652
  118.9 20.9 %copy-start.86 = (f32[12,256]{1,0:T(8,128)}, f32[12,256]{1,0:T(8,128)S(1)}, u32[]{:S(2)}) copy-start(f32[12,256]{1,0:T(8,128)S(1)} %add_divide_fusion.1) | copy-start | bytes 36868
  129.9 6.2 copy-start.2
  129.9 6.2 copy-start.31
  130.0 12.5 slice-start.17
  136.2 6.3 slice-start.18
  136.2 6.3 slice-start.19
  150.5 166.2 %reduce-scatter.19.cloned.1.call-start = ((), (), s32[]{:S(2)}) async-start(), calls=%async_computation.12 | async-start | bytes 7864320 | tf_op jit(solution)/shard_map/reduce_scatter | solution.py:194
  153.5 54.8 %copy-start.73 = (bf16[256,768]{0,1:T(8,128)(2,1)}, bf16[256,768]{0,1:T(8,128)(2,1)S(1)}, u32[]{:S(2)}) copy-start(bf16[256,768]{0,1:T(8,128)(2,1)S(1)} %copy.87) | copy-start | bytes 1179652
  154.9 97.2 %copy-start.22 = (bf16[256,768]{0,1:T(8,128)(2,1)}, bf16[256,768]{0,1:T(8,128)(2,1)S(1)}, u32[]{:S(2)}) copy-start(bf16[256,768]{0,1:T(8,128)(2,1)S(1)} %copy.85) | copy-start | bytes 1179652
  194.7 8.3 copy-start.3
  194.7 16.4 %slice-start.20 = ((s8[9437184]{0:T(1024)(128)(4,1)}), s8[4194304]{0:T(1024)(128)(4,1)S(1)}, s32[]{:S(2)}) async-start(s8[9437184]{0:T(1024)(128)(4,1)} %bitcast.434), calls=%async_computation.44 | async-start | bytes 8388608
  203.0 8.1 slice-start.21
  203.0 8.1 slice-start.22
  210.8 175.3 %copy-start.12 = (f32[256,768]{1,0:T(8,128)}, f32[256,768]{1,0:T(8,128)S(1)}, u32[]{:S(2)}) copy-start(f32[256,768]{1,0:T(8,128)S(1)} %get-tuple-element.129) | copy-start | bytes 2359300
  212.6 6.2 copy-start.35
  226.5 10.9 copy-start.61
  226.5 18.6 %slice-start.3 = ((s8[12582912]{0:T(1024)(128)(4,1)}), s8[4194304]{0:T(1024)(128)(4,1)S(1)}, s32[]{:S(2)}) async-start(s8[12582912]{0:T(1024)(128)(4,1)} %bitcast.348), calls=%async_computation.27 | async-start | bytes 8388608
  226.5 18.6 %slice-start.4 = ((s8[12582912]{0:T(1024)(128)(4,1)}), s8[4194304]{0:T(1024)(128)(4,1)S(1)}, s32[]{:S(2)}) async-start(s8[12582912]{0:T(1024)(128)(4,1)} %bitcast.348), calls=%async_computation.28 | async-start | bytes 8388608
  237.4 7.6 slice-start.5
  258.1 167.1 %reduce-scatter.21.cloned.1.call-start = ((), (), s32[]{:S(2)}) async-start(), calls=%async_computation.13 | async-start | bytes 7864320 | tf_op jit(solution)/shard_map/reduce_scatter | solution.py:194
  258.3 7.2 slice-start.8
  259.1 6.3 slice-start.9
  267.5 55.1 %copy-start.49 = (bf16[12,64,256]{2,1,0:T(8,128)(2,1)}, bf16[12,64,256]{2,1,0:T(8,128)(2,1)S(1)}, u32[]{:S(2)}) copy-start(bf16[12,64,256]{2,1,0:T(8,128)(2,1)S(1)} %fusion.152) | copy-start | bytes 1179652
  318.2 12.0 slice-start.23
  323.0 7.2 slice-start.24
  324.5 7.8 copy-start.24
  324.5 5.7 slice-start.25
  333.6 34.9 %copy-start.10 = (f32[256,768]{1,0:T(8,128)}, f32[256,768]{1,0:T(8,128)S(1)}, u32[]{:S(2)}) copy-start(f32[256,768]{1,0:T(8,128)S(1)} %add_add_fusion.5) | copy-start | bytes 2359300
  335.0 11.2 copy-start.64
  335.0 18.8 %slice-start = ((s8[12582912]{0:T(1024)(128)(4,1)}), s8[4194304]{0:T(1024)(128)(4,1)S(1)}, s32[]{:S(2)}) async-start(s8[12582912]{0:T(1024)(128)(4,1)} %bitcast.346), calls=%async_computation.24 | async-start | bytes 8388608
  335.0 18.8 %slice-start.1 = ((s8[12582912]{0:T(1024)(128)(4,1)}), s8[4194304]{0:T(1024)(128)(4,1)S(1)}, s32[]{:S(2)}) async-start(s8[12582912]{0:T(1024)(128)(4,1)} %bitcast.346), calls=%async_computation.25 | async-start | bytes 8388608
  346.1 7.7 slice-start.2
  353.8 6.9 copy-start.21
  366.7 109.5 %reduce-scatter.25.cloned.1.call-start = ((), (), s32[]{:S(2)}) async-start(), calls=%async_computation.15 | async-start | bytes 5898240 | tf_op jit(solution)/shard_map/reduce_scatter | solution.py:241
  371.5 246.9 %reduce-scatter.29.cloned.1.call-start = ((), (), s32[]{:S(2)}) async-start(), calls=%async_computation.17 | async-start | bytes 23592960 | tf_op jit(solution)/shard_map/reduce_scatter | solution.py:243
  386.0 374.6 %reduce-scatter.27.cloned.1.call-start = ((), (), s32[]{:S(2)}) async-start(), calls=%async_computation.16 | async-start | bytes 23592960 | tf_op jit(solution)/shard_map/reduce_scatter | solution.py:242
  397.9 474.9 %reduce-scatter.23.cloned.1.call-start = ((), (), s32[]{:S(2)}) async-start(), calls=%async_computation.14 | async-start | bytes 17694720 | tf_op jit(solution)/shard_map/reduce_scatter | solution.py:240
  402.4 6.8 copy-start.6
  416.3 10.5 copy-start.51
  416.3 10.5 copy-start.18
  416.3 10.5 copy-start.77
  416.3 10.5 copy-start.83
  416.3 10.5 copy-start.85
  448.0 446.7 %reduce-scatter.37.cloned.1.call-start = ((), (), s32[]{:S(2)}) async-start(), calls=%async_computation.21 | async-start | bytes 163840
  453.3 463.5 %reduce-scatter.35.cloned.1.call-start = ((), (), s32[]{:S(2)}) async-start(), calls=%async_computation.20 | async-start | bytes 163840
  454.2 486.4 %reduce-scatter.33.cloned.1.call-start = ((), (), s32[]{:S(2)}) async-start(), calls=%async_computation.19 | async-start | bytes 491520
  455.2 509.2 %reduce-scatter.31.cloned.1.call-start = ((), (), s32[]{:S(2)}) async-start(), calls=%async_computation.18 | async-start | bytes 491520
  460.5 948.9 %all-reduce.7.cloned.1.call-start = ((), (), s32[]{:S(2)}) async-start(), calls=%async_computation.22 | async-start | bytes 28311552 | tf_op jit(solution)/shard_map/psum | solution.py:249
  873.9 67.6 %copy-start.11 = (f32[256,768]{1,0:T(8,128)S(1)}, f32[256,768]{1,0:T(8,128)}, u32[]{:S(2)}) copy-start(f32[256,768]{1,0:T(8,128)} %copy-done.10) | copy-start | bytes 2359300
  (78 other events, 218.6 us)
Sparse Core Ops, SparseCore 0:
  11.0 38.8 all-reduce.8
  52.2 28.9 all-gather.2
  150.6 28.9 all-gather.4
  258.3 58.3 reduce-scatter.18
  366.9 58.3 reduce-scatter.20
  428.4 47.8 reduce-scatter.24
  478.9 139.4 reduce-scatter.28
  621.1 139.4 reduce-scatter.26
  763.2 109.4 reduce-scatter.22
  875.0 19.5 reduce-scatter.36
  897.2 19.5 reduce-scatter.34
  919.7 20.7 reduce-scatter.32
  943.6 20.7 reduce-scatter.30
  969.0 440.3 all-reduce.6
where the time goes:
time: 1430 us
  waiting for transfers between devices  1010 us (71%)
  matrix products  156 us (11%)
  other arithmetic  141 us (10%)
  local copies, waits for them, and re-layouts  73.9 us (5%)
  blocking collectives  22.7 us (2%)
  between operations  18.3 us (1%)
    psum x1, waiting for transfers between devices, on_device(): lax.psum((shares[0], shares[1], shares[2], shares[3], shares[4], shares[5...  421 us
    reduce_scatter x1, waiting for transfers between devices, on_device(): lax.psum_scatter(jnp.stack(grads_up), 'blk', scatter_dimension=1, tiled=T...  142 us
    reduce_scatter x1, waiting for transfers between devices, on_device(): lax.psum_scatter(jnp.stack(grads_down), 'blk', scatter_dimension=1, tiled...  142 us
    reduce_scatter x1, waiting for transfers between devices, on_device(): lax.psum_scatter(jnp.stack(grads_qkv), 'blk', scatter_dimension=1, tiled=...  112 us
    unnamed x18, waiting for transfers between devices  80.9 us
    reduce_scatter x2, waiting for transfers between devices, on_device(): d_kv = lax.psum_scatter(whole_terms, 'blk', scatter_dimension=0, tiled=True)  54.7 us
    unnamed x266, local copies, waits for them, and re-layouts  38 us
    another operation x6, other arithmetic, on_device(): factor = jnp.linalg.cholesky(gram)  34 us
  transfers between devices with their start and end apart: 14, of which 13 were waited for; matrix products, arithmetic and copies ran while one was open for 13% of the time, Pallas kernels for 0%

commit v1 on v0

v1 whole, which is shorter than its diff:
```python
import jax
import jax.numpy as jnp
from jax import lax
from jax.sharding import PartitionSpec as P

HEADS = 12
HEAD = 64
D = 768
NBASIS = 256
LAYERS = 2
MEMPOS = 4096

highest = lax.Precision.HIGHEST
ridge_weight = 0.5
bf16 = jnp.bfloat16
f32 = jnp.float32


def dot32(a, b):
    return jnp.dot(a, b, preferred_element_type=f32)


def layer_norm(inputs, gain):
    average = jnp.mean(inputs, axis=-1, keepdims=True)
    centred = inputs - average
    spread = jnp.mean(centred * centred, axis=-1, keepdims=True)
    return centred * lax.rsqrt(spread + 1e-05) * gain


def centres_of(count):
    return (jnp.arange(count).astype(f32) + 0.5) / count


def density(scores, weight_mu, weight_sig):
    count = scores.shape[-1]
    breadth = 1.0 / count
    place = jax.nn.sigmoid(jnp.sum(scores * weight_mu, axis=-1, keepdims=True))
    variance = (0.5 + jax.nn.softplus(jnp.sum(scores * weight_sig, axis=-1, keepdims=True))) / 64.0
    offset = place - centres_of(count)
    return jnp.sqrt(breadth * breadth / variance) * jnp.exp(-offset * offset / (2.0 * variance))


def basis_table(positions):
    breadth = 1.0 / NBASIS
    times = (positions.astype(f32) + 0.5) / MEMPOS
    offset = times[:, None] - centres_of(NBASIS)[None, :]
    return jnp.exp(-offset * offset / (2.0 * breadth * breadth))


def gelu_piece(upward):
    return jax.nn.gelu(upward, approximate=True)


def masked_scores(query, keys, allowed, scale):
    scores = jnp.einsum("qhd,khd->hqk", query, keys, preferred_element_type=f32) * scale
    return jnp.where(allowed[None], scores, -1e30)


def swap(value, axis, bit):
    count = lax.axis_size(axis)
    return lax.ppermute(value, axis, [(i, i ^ bit) for i in range(count)])


def bits_of(axis):
    return [1 << i for i in range(lax.axis_size(axis).bit_length() - 1)]


def relative_gather(value, axis):
    held = {0: value}
    for bit in reversed(bits_of(axis)):
        held.update({k | bit: swap(v, axis, bit) for k, v in list(held.items())})
    return [held[k] for k in range(lax.axis_size(axis))]


def relative_scatter(parts, axis):
    held = dict(enumerate(parts))
    for bit in bits_of(axis):
        sent = {k: swap(v, axis, bit) for k, v in held.items() if k & bit}
        held = {
            k: (v.astype(f32) + sent[k | bit].astype(f32)).astype(bf16)
            for k, v in held.items()
            if not k & bit
        }
    return held[0]


def split_order(count):
    width = count.bit_length() - 1
    return [int(format(k, "b").zfill(width)[::-1], 2) if width else 0 for k in range(count)]


def shard_columns(left, axis):
    count = lax.axis_size(axis)
    own = lax.axis_index(axis)
    size = left.shape[1] // count
    return [
        lax.dynamic_slice_in_dim(left, jnp.bitwise_xor(own, k) * size, size, axis=1)
        for k in split_order(count)
    ]


def reduce_weight(left, right):
    pieces = shard_columns(left, "blk")
    half = len(pieces) // 2
    keep = jnp.concatenate(pieces[:half], 1)
    send = jnp.concatenate(pieces[half:], 1)
    bits = bits_of("blk")
    got = swap(dot32(send.T, right).astype(bf16), "blk", bits[0])
    total = (dot32(keep.T, right) + got.astype(f32)).astype(bf16)
    for bit in bits[1:]:
        rows = total.shape[0] // 2
        got = swap(total[rows:], "blk", bit)
        total = (total[:rows].astype(f32) + got.astype(f32)).astype(bf16)
    own = lax.axis_index("batch")
    bits = bits_of("batch")
    for bit in bits:
        rows = total.shape[0] // 2
        side = jnp.where(jnp.bitwise_and(own, bit) > 0, rows, 0)
        got = swap(lax.dynamic_slice_in_dim(total, rows - side, rows, 0), "batch", bit)
        kept = lax.dynamic_slice_in_dim(total, side, rows, 0)
        total = (kept.astype(f32) + got.astype(f32)).astype(bf16)
    for bit in reversed(bits):
        got = swap(total, "batch", bit)
        upper = jnp.bitwise_and(own, bit) > 0
        total = jnp.concatenate([jnp.where(upper, got, total), jnp.where(upper, total, got)], 0)
    return total.astype(f32)


def on_device(
    tokens,
    memory,
    mem_pos,
    seg_count,
    w_qkv,
    w_out,
    w_up,
    w_down,
    gain_attn,
    gain_mlp,
    w_mu,
    w_sig,
    cotangent,
):
    rows = tokens.shape[0]
    width = D
    heads = HEADS
    head = HEAD
    count = lax.axis_size("blk")
    seq = rows * count
    scale = HEAD ** (-0.5)
    length = seg_count[0] * rows
    own = lax.axis_index("blk")
    own_places = own * rows + jnp.arange(rows, dtype=jnp.int32)
    all_places = jnp.concatenate(
        [jnp.bitwise_xor(own, k) * rows + jnp.arange(rows, dtype=jnp.int32) for k in range(count)]
    )
    allowed = (all_places[None, :] <= own_places[:, None]) & (all_places[None, :] < length)
    places = jnp.concatenate(relative_gather(mem_pos[0], "blk"), 0)
    samples = jnp.concatenate(relative_gather(memory[0], "blk"), 0).astype(f32)
    basis = basis_table(places)
    gram = jnp.dot(basis.T, basis, precision=highest)
    right = jnp.dot(basis.T, samples, precision=highest)
    gram = gram + ridge_weight * jnp.eye(NBASIS, dtype=f32)
    factor = jnp.linalg.cholesky(gram)
    coeff_low = jax.scipy.linalg.cho_solve((factor, True), right).astype(bf16)
    hidden = tokens.astype(f32)
    saved = []
    for layer in range(LAYERS):
        normed = layer_norm(hidden, gain_attn[layer]).astype(bf16)
        normed_all = jnp.concatenate(relative_gather(normed, "blk"), 0)
        query = dot32(normed, w_qkv[layer][:, :width]).astype(bf16).reshape(rows, heads, head)
        kv_whole = dot32(normed_all, w_qkv[layer][:, width:]).astype(bf16)
        keys = kv_whole[:, :width].reshape(seq, heads, head)
        values = kv_whole[:, width:].reshape(seq, heads, head)
        scores = masked_scores(query, keys, allowed, scale)
        peak = jnp.max(scores, axis=-1, keepdims=True)
        expo = jnp.exp(scores - peak)
        total = jnp.sum(expo, axis=-1, keepdims=True)
        probs = (expo / total).astype(bf16)
        log_total = peak + jnp.log(total)
        local = jnp.einsum("hqk,khd->qhd", probs, values, preferred_element_type=f32)
        memory_kv = dot32(coeff_low, w_qkv[layer][:, width:]).astype(bf16)
        mem_keys = memory_kv[:, :width].reshape(NBASIS, heads, head)
        mem_values = memory_kv[:, width:].reshape(NBASIS, heads, head)
        mem_scores = (
            jnp.einsum("qhd,nhd->hqn", query, mem_keys, preferred_element_type=f32) * scale
        )
        weights = density(mem_scores, w_mu[layer], w_sig[layer]).astype(bf16)
        recalled = jnp.einsum("hqn,nhd->qhd", weights, mem_values, preferred_element_type=f32)
        attended = (local + recalled).reshape(rows, width).astype(bf16)
        middle = hidden + dot32(attended, w_out[layer])
        normed2 = layer_norm(middle, gain_mlp[layer]).astype(bf16)
        upward = dot32(normed2, w_up[layer])
        active = gelu_piece(upward).astype(bf16)
        saved.append(
            (
                hidden,
                normed,
                normed_all,
                query,
                keys,
                values,
                log_total,
                mem_keys,
                mem_values,
                attended,
                middle,
                normed2,
                upward,
                active,
            )
        )
        hidden = middle + dot32(active, w_down[layer])
    live = (own_places < length).astype(f32)[:, None]
    grad = cotangent.astype(f32) * live
    results = [None] * LAYERS
    small = [None] * LAYERS
    for layer in reversed(range(LAYERS)):
        (
            layer_input,
            normed,
            normed_all,
            query,
            keys,
            values,
            log_total,
            mem_keys,
            mem_values,
            attended,
            middle,
            normed2,
            upward,
            active,
        ) = saved[layer]
        grad_low = grad.astype(bf16)
        d_down = reduce_weight(active, grad_low)
        d_active = dot32(grad_low, w_down[layer].T)
        unused, gelu_back = jax.vjp(gelu_piece, upward)
        d_upward = gelu_back(d_active)[0].astype(bf16)
        d_up = reduce_weight(normed2, d_upward)
        d_normed2 = dot32(d_upward, w_up[layer].T)
        unused, norm_back = jax.vjp(layer_norm, middle, gain_mlp[layer])
        d_middle, d_gain_mlp = norm_back(d_normed2)
        grad = grad + d_middle
        grad_low = grad.astype(bf16)
        d_out = reduce_weight(attended, grad_low)
        d_attended = dot32(grad_low, w_out[layer].T).astype(bf16)
        d_heads = d_attended.reshape(rows, heads, head)
        scores = masked_scores(query, keys, allowed, scale)
        probs = jnp.exp(scores - log_total)
        probs_low = probs.astype(bf16)
        d_probs = jnp.einsum("qhd,khd->hqk", d_heads, values, preferred_element_type=f32)
        correction = jnp.sum(probs * d_probs, axis=-1, keepdims=True)
        d_scores = (probs * (d_probs - correction)).astype(bf16)
        d_query = jnp.einsum("hqk,khd->qhd", d_scores, keys, preferred_element_type=f32)
        d_keys = jnp.einsum("hqk,qhd->khd", d_scores, query, preferred_element_type=f32)
        d_values = jnp.einsum("hqk,qhd->khd", probs_low, d_heads, preferred_element_type=f32)
        mem_scores = (
            jnp.einsum("qhd,nhd->hqn", query, mem_keys, preferred_element_type=f32) * scale
        )
        weights, density_back = jax.vjp(density, mem_scores, w_mu[layer], w_sig[layer])
        weights_low = weights.astype(bf16)
        d_weights = jnp.einsum("qhd,nhd->hqn", d_heads, mem_values, preferred_element_type=f32)
        d_mem_values = jnp.einsum("hqn,qhd->nhd", weights_low, d_heads, preferred_element_type=f32)
        d_mem_scores, d_mu, d_sig = density_back(d_weights)
        d_mem_low = d_mem_scores.astype(bf16)
        d_query = d_query + jnp.einsum(
            "hqn,nhd->qhd", d_mem_low, mem_keys, preferred_element_type=f32
        )
        d_mem_keys = jnp.einsum("hqn,qhd->nhd", d_mem_low, query, preferred_element_type=f32)
        d_query = (d_query * scale).reshape(rows, width).astype(bf16)
        d_kv = jnp.concatenate(
            [(d_keys * scale).reshape(seq, width), d_values.reshape(seq, width)], 1
        ).astype(bf16)
        d_memory_kv = jnp.concatenate(
            [(d_mem_keys * scale).reshape(NBASIS, width), d_mem_values.reshape(NBASIS, width)], 1
        ).astype(bf16)
        d_normed_terms = dot32(d_kv, w_qkv[layer][:, width:].T)
        d_normed_terms = d_normed_terms + jnp.pad(
            dot32(d_query, w_qkv[layer][:, :width].T), ((0, seq - rows), (0, 0))
        )
        d_normed_terms = d_normed_terms.astype(bf16).reshape(count, rows, width)
        d_normed = relative_scatter([d_normed_terms[k] for k in range(count)], "blk").astype(f32)
        d_kv_weight = reduce_weight(
            jnp.concatenate([normed_all, coeff_low], 0), jnp.concatenate([d_kv, d_memory_kv], 0)
        )
        d_q_weight = reduce_weight(normed, d_query)
        unused, norm_back = jax.vjp(layer_norm, layer_input, gain_attn[layer])
        d_input, d_gain_attn = norm_back(d_normed)
        grad = grad + d_input
        results[layer] = (jnp.concatenate([d_q_weight, d_kv_weight], 1), d_out, d_up, d_down)
        small[layer] = (d_gain_attn, d_gain_mlp, d_mu, d_sig)
    sizes = [item.shape[0] for item in small[0]]
    packed = jnp.concatenate([item for layer in small for item in layer])
    packed = lax.psum(packed, ("batch", "blk")).reshape(LAYERS, sum(sizes))
    shares = []
    first = 0
    for size in sizes:
        share = size // count
        shares.append(lax.dynamic_slice_in_dim(packed, first + own * share, share, 1))
        first += size
    return (
        hidden.astype(bf16),
        grad,
        *[jnp.stack([results[layer][i] for layer in range(LAYERS)]) for i in range(4)],
        *shares,
    )


def solution(mesh):
    placed = (
        P(("batch", "blk"), None),
        P("batch", "blk", None),
        P("batch", "blk"),
        P("batch"),
        P(),
        P(),
        P(),
        P(),
        P(),
        P(),
        P(),
        P(),
        P(("batch", "blk"), None),
    )
    return jax.shard_map(
        on_device,
        mesh=mesh,
        in_specs=placed,
        out_specs=(
            P(("batch", "blk"), None),
            P(("batch", "blk"), None),
            P(None, "blk", None),
            P(None, "blk", None),
            P(None, "blk", None),
            P(None, "blk", None),
            P(None, "blk"),
            P(None, "blk"),
            P(None, "blk"),
            P(None, "blk"),
        ),
        check_vma=False,
    )
```

time: 1430 us -> 744 us (0.52)
  waiting for transfers between devices: 1010 us -> 229 us
  starting transfers between devices: 0.87 us -> 102 us
  blocking collectives: 22.7 us -> 52.4 us
  other arithmetic: 141 us -> 114 us
    reduce_scatter x6 -> x0, waiting for transfers between devices: 467 us -> none  [the longest x1 142 us: on_device(): lax.psum_scatter(jnp.stack(grads_up), 'blk', scatter_dimension=1, tiled=T...]
    psum x2 -> x0, waiting for transfers between devices: 444 us -> none  [the longest x1 421 us: on_device(): lax.psum((shares[0], shares[1], shares[2], shares[3], shares[4], shares[5...]
    ppermute x0 -> x98, waiting for transfers between devices: none -> 229 us  [swap(): return lax.ppermute(value, axis, [(i, i ^ bit) for i in range(count)])]
    ppermute x0 -> x98, starting transfers between devices: none -> 102 us  [swap(): return lax.ppermute(value, axis, [(i, i ^ bit) for i in range(count)])]
    unnamed x18 -> x0, waiting for transfers between devices: 80.9 us -> none
    psum x1, blocking collectives: 22.7 us -> 52.4 us  [on_device(): packed = lax.psum(packed, ('batch', 'blk')).reshape(LAYERS, sum(sizes))]
    another operation x15 -> x9, other arithmetic: 59.4 us -> 29.9 us  [the longest x3 21.1 us: on_device(): coeff_low = jax.scipy.linalg.cho_solve((factor, True), right).astype(bf16)]
    all_gather x2 -> x0, waiting for transfers between devices: 22.3 us -> none  [on_device(): kv_whole = lax.all_gather(qkv[:, width:], 'blk', axis=0, tiled=True)]
  transfers between devices with their start and end apart: 14 -> 98, of which waited for: 13 -> 56; matrix products, arithmetic and copies ran while one was open for 13% -> 30% of each run, Pallas kernels for 0% -> 0%
where the time goes in v1:
time: 744 us; the launch traced here: 734 us
  waiting for transfers between devices  229 us (31%)
  matrix products  153 us (21%)
  other arithmetic  114 us (15%)
  starting transfers between devices  102 us (14%)
  local copies, waits for them, and re-layouts  76.5 us (10%)
  blocking collectives  52.4 us (7%)
    ppermute x98, waiting for transfers between devices, swap(): return lax.ppermute(value, axis, [(i, i ^ bit) for i in range(count)])  229 us
    ppermute x98, starting transfers between devices, swap(): return lax.ppermute(value, axis, [(i, i ^ bit) for i in range(count)])  102 us
    dot_general x42, matrix products, dot32(): return jnp.dot(a, b, preferred_element_type=f32)  78.3 us
    psum x1, blocking collectives, on_device(): packed = lax.psum(packed, ('batch', 'blk')).reshape(LAYERS, sum(sizes))  52.4 us
    another operation x6, other arithmetic, on_device(): factor = jnp.linalg.cholesky(gram)  34.1 us
    another operation x3, other arithmetic, on_device(): coeff_low = jax.scipy.linalg.cho_solve((factor, True), right).astype(bf16)  21.1 us
    unnamed x454, local copies, waits for them, and re-layouts  18.3 us
  transfers between devices with their start and end apart: 98, of which 56 were waited for; matrix products, arithmetic and copies ran while one was open for 30% of the time, Pallas kernels for 0%

profile of v1, /device:TPU:0, one launch (start us, length us, event | category | flops | bytes accessed | tf_op | source)
XLA Modules:
  0.0 734.2 jit_solution(9474114866967654423)
XLA Ops:
  15.2 5.3 slice_bitcast_fusion
  28.8 11.7 %cholesky.49 = f32[128,128]{1,0:T(8,128)S(1)} custom-call(f32[128,128]{1,0:T(8,128)S(1)} %cholesky.115), custom_call_target="Cholesky" | custom-call | tf_op jit(solution)/shard_map/jit(cholesky)/cholesky | solution.py:164
  40.6 9.8 %custom-call.18 = f32[1,128,128]{1,2,0:T(8,128)S(1)} custom-call(f32[1,128,128]{2,1,0:T(8,128)S(1)} %get-tuple-element.201), custom_call_target="InvertDiagBlocksLowerTriangular" | custom-call | tf_op jit(solution)/shard_map/jit(cholesky)/cholesky | solution.py:164
  52.6 11.9 %cholesky.103 = f32[128,128]{1,0:T(8,128)S(1)} custom-call(f32[128,128]{1,0:T(8,128)S(1)} %convolution_subtract_fusion.1), custom_call_target="Cholesky" | custom-call | tf_op jit(solution)/shard_map/jit(cholesky)/cholesky | solution.py:164
  67.5 5.2 while.1
  72.7 20.5 %custom-call.19 = f32[2,128,128]{1,2,0:T(8,128)S(1)} custom-call(f32[2,128,128]{2,1,0:T(8,128)} %get-tuple-element.25), custom_call_target="InvertDiagBlocksLowerTriangular" | custom-call | tf_op jit(solution)/shard_map/jit(_cho_solve)/triangular_solve | solution.py:165
  109.5 4.6 convolution_convert_fusion.3
  117.7 3.5 copy.62
  123.6 3.7 fusion
  129.8 3.6 fusion.10
  137.4 3.5 multiply_convert_fusion.7
  164.6 3.7 convolution_convert_fusion.2
  176.8 3.9 fusion.1
  183.1 3.6 fusion.11
  196.6 3.4 fusion.73
  215.8 4.5 fusion.98
  220.3 7.4 %multiply_reduce_fusion.1 = (f32[12,256]{1,0:T(8,128)S(1)}, f32[12,256,1024]{2,1,0:T(8,128)}) fusion(f32[12,256]{1,0:T(8,128)S(1)} %copy-done.122, f32[12,256,1024]{2,1,0:T(8,128)S(1)} %bitcast.359, pred[256,1024]{1,0:T(8,128)(4,1)S(1)} %compare_and_fusion, bf16[256,12,64]{0,2,1:T(8,128)(2,1)S(1)} %bitcast.401, bf16[1024,12,64]{0,2,1:T(8,128)(2,1)S(1)} %bitcast.381), kind=kOutput, calls=%fused_computation.6 | convolution fusion | flops 418378752 | bytes 27418624 | tf_op jit(solution)/shard_map/qhd,khd->hqk/dot_general | solution.py:252
  237.0 6.9 multiply_convert_fusion.1
  261.2 7.4 %collective-permute-done.14 = bf16[256,768]{1,0:T(8,128)(2,1)S(1)} collective-permute-done((bf16[256,768]{1,0:T(8,128)(2,1)S(1)}, bf16[256,768]{1,0:T(8,128)(2,1)S(1)}, u32[]{:S(2)}, u32[]{:S(2)}) %collective-permute-start.14) | collective-permute-done | bytes 393248 | tf_op jit(solution)/shard_map/ppermute | solution.py:61
  271.7 3.2 fusion.66
  290.6 4.5 fusion.101
  295.1 7.4 %multiply_reduce_fusion = (f32[12,256]{1,0:T(8,128)S(1)}, f32[12,256,1024]{2,1,0:T(8,128)}) fusion(f32[12,256]{1,0:T(8,128)S(1)} %copy-done.121, f32[12,256,1024]{2,1,0:T(8,128)S(1)} %bitcast.357, pred[256,1024]{1,0:T(8,128)(4,1)S(1)} %compare_and_fusion, bf16[256,12,64]{0,2,1:T(8,128)(2,1)S(1)} %bitcast.397, bf16[1024,12,64]{0,2,1:T(8,128)(2,1)S(1)} %bitcast.379), kind=kOutput, calls=%fused_computation.3 | convolution fusion | flops 418378752 | bytes 27418624 | tf_op jit(solution)/shard_map/qhd,khd->hqk/dot_general | solution.py:252
  302.5 7.1 multiply_convert_fusion
  321.4 3.1 convolution_convert_fusion.7
  330.7 3.5 collective-permute-done.60
  335.8 3.7 collective-permute-done.36
  345.5 3.1 collective-permute-done.37
  369.0 3.3 add_convert_fusion.12
  377.8 3.3 collective-permute-done.40
  386.1 3.2 collective-permute-done.65
  391.8 3.2 collective-permute-done.41
  398.3 52.4 %psum.7 = f32[2,2048]{1,0:T(2,128)S(1)} all-reduce(f32[2,2048]{1,0:T(2,128)S(1)} %reshape.743), channel_id=1, replica_groups=mesh['batch'=8,'blk'=4] {'batch','blk'}, use_global_device_ids=true, to_apply=%region_44.46 | all-reduce | flops 4096 | bytes 32768 | tf_op jit(solution)/shard_map/psum | solution.py:295
  456.8 4.6 collective-permute-done.19
  464.1 3.7 collective-permute-done.52
  469.2 4.1 collective-permute-done.20
  473.6 4.1 collective-permute-done.53
  477.9 4.2 collective-permute-done.21
  482.3 5.0 collective-permute-done.54
  487.6 4.6 collective-permute-done.22
  492.5 3.5 add_convert_fusion.13
  498.9 3.9 collective-permute-done.23
  503.3 4.0 collective-permute-done.56
  507.7 4.0 collective-permute-done.24
  513.0 7.0 collective-permute-done.44
  521.3 3.8 collective-permute-done.57
  525.5 4.8 collective-permute-done.45
  531.6 3.8 collective-permute-done.25
  536.3 5.0 collective-permute-done.46
  542.9 3.7 collective-permute-done.47
  554.3 8.6 %collective-permute-done.27 = bf16[192,1536]{1,0:T(8,128)(2,1)S(1)} collective-permute-done((bf16[192,1536]{1,0:T(8,128)(2,1)S(1)}, bf16[192,1536]{1,0:T(8,128)(2,1)S(1)}, u32[]{:S(2)}, u32[]{:S(2)}) %collective-permute-start.27) | collective-permute-done | bytes 589856 | tf_op jit(solution)/shard_map/ppermute | solution.py:61
  566.7 4.8 collective-permute-done.28
  571.7 5.1 collective-permute-done.29
  578.7 8.0 %collective-permute-done.49 = bf16[96,1536]{1,0:T(8,128)(2,1)S(1)} collective-permute-done((bf16[96,1536]{1,0:T(8,128)(2,1)S(1)}, bf16[96,1536]{1,0:T(8,128)(2,1)S(1)}, u32[]{:S(2)}, u32[]{:S(2)}) %collective-permute-start.49) | collective-permute-done | bytes 294944 | tf_op jit(solution)/shard_map/ppermute | solution.py:61
  587.6 4.8 collective-permute-done.30
  592.9 5.0 collective-permute-done.31
  606.7 6.7 collective-permute-done.91
  619.4 10.7 %collective-permute-done.92 = bf16[384,768]{1,0:T(8,128)(2,1)S(1)} collective-permute-done((bf16[384,768]{1,0:T(8,128)(2,1)S(1)}, bf16[384,768]{1,0:T(8,128)(2,1)S(1)}, u32[]{:S(2)}, u32[]{:S(2)}) %collective-permute-start.92) | collective-permute-done | bytes 589856 | tf_op jit(solution)/shard_map/ppermute | solution.py:61
  630.6 8.1 %collective-permute-done.67 = bf16[192,3072]{1,0:T(8,128)(2,1)S(1)} collective-permute-done((bf16[192,3072]{1,0:T(8,128)(2,1)S(1)}, bf16[192,3072]{1,0:T(8,128)(2,1)S(1)}, u32[]{:S(2)}, u32[]{:S(2)}) %collective-permute-start.67) | collective-permute-done | bytes 1179680 | tf_op jit(solution)/shard_map/ppermute | solution.py:61
  640.7 11.0 %collective-permute-done.83 = bf16[768,768]{1,0:T(8,128)(2,1)S(1)} collective-permute-done((bf16[768,768]{1,0:T(8,128)(2,1)S(1)}, bf16[768,768]{1,0:T(8,128)(2,1)S(1)}, u32[]{:S(2)}, u32[]{:S(2)}) %collective-permute-start.83) | collective-permute-done | bytes 1179680 | tf_op jit(solution)/shard_map/ppermute | solution.py:61
  656.7 3.9 collective-permute-done.78
  679.1 5.8 collective-permute-done.96
  691.9 3.5 collective-permute-done.85
  718.9 5.8 collective-permute-done.73
  727.7 3.3 collective-permute-done.89
  (934 shorter events, 338.1 us)
Async XLA Ops:
  0.6 24.3 %collective-permute-start.4 = (s32[128]{0:T(128)}, s32[128]{0:T(128)S(1)}, u32[]{:S(2)}, u32[]{:S(2)}) collective-permute-start(s32[128]{0:T(128)} %bitcast.420), channel_id=1, source_target_pairs={{0,2},{1,3},{2,0},{3,1},{4,6},{5,7},{6,4},{7,5},{8,10},{9,11},{10,... | collective-permute-start | bytes 1544 | tf_op jit(solution)/shard_map/ppermute | solution.py:61
  3.6 21.4 %collective-permute-start.3 = (s32[128]{0:T(128)}, s32[128]{0:T(128)S(1)}, u32[]{:S(2)}, u32[]{:S(2)}) collective-permute-start(s32[128]{0:T(128)} %bitcast.421), channel_id=1, source_target_pairs={{0,1},{1,0},{2,3},{3,2},{4,5},{5,4},{6,7},{7,6},{8,9},{9,8},{10,11... | collective-permute-start | bytes 1544 | tf_op jit(solution)/shard_map/ppermute | solution.py:61
  3.6 62.8 %collective-permute-start.7 = (bf16[128,768]{1,0:T(8,128)(2,1)}, bf16[128,768]{1,0:T(8,128)(2,1)}, u32[]{:S(2)}, u32[]{:S(2)}) collective-permute-start(bf16[128,768]{1,0:T(8,128)(2,1)} %bitcast.435), channel_id=1, source_target_pairs={{0,2},{1,3},{2,0},{3,1},{4,6},{5,7},{6,4},{7,5},{8,10},{9,11},{10,... | collective-permute-start | bytes 589832 | tf_op jit(solution)/shard_map/ppermute | solution.py:61
  3.8 89.4 %collective-permute-start.6 = (bf16[128,768]{1,0:T(8,128)(2,1)}, bf16[128,768]{1,0:T(8,128)(2,1)}, u32[]{:S(2)}, u32[]{:S(2)}) collective-permute-start(bf16[128,768]{1,0:T(8,128)(2,1)} %bitcast.436), channel_id=1, source_target_pairs={{0,1},{1,0},{2,3},{3,2},{4,5},{5,4},{6,7},{7,6},{8,9},{9,8},{10,11... | collective-permute-start | bytes 589832 | tf_op jit(solution)/shard_map/ppermute | solution.py:61
  8.6 87.9 %collective-permute-start.1 = (bf16[256,768]{1,0:T(8,128)(2,1)S(1)}, bf16[256,768]{1,0:T(8,128)(2,1)}, u32[]{:S(2)}, u32[]{:S(2)}) collective-permute-start(bf16[256,768]{1,0:T(8,128)(2,1)S(1)} %get-tuple-element.71), channel_id=1, source_target_pairs={{0,2},{1,3},{2,0},{3,1},{4,6},{5,7},{6,4},{7,5},{8,10},{9,11},{10,... | collective-permute-start | bytes 1179656 | tf_op jit(solution)/shard_map/ppermute | solution.py:61
  25.0 72.8 %collective-permute-start = (bf16[256,768]{1,0:T(8,128)(2,1)S(1)}, bf16[256,768]{1,0:T(8,128)(2,1)}, u32[]{:S(2)}, u32[]{:S(2)}) collective-permute-start(bf16[256,768]{1,0:T(8,128)(2,1)S(1)} %get-tuple-element.71), channel_id=1, source_target_pairs={{0,1},{1,0},{2,3},{3,2},{4,5},{5,4},{6,7},{7,6},{8,9},{9,8},{10,11... | collective-permute-start | bytes 1179656 | tf_op jit(solution)/shard_map/ppermute | solution.py:61
  66.5 26.7 %collective-permute-start.8 = (bf16[128,768]{1,0:T(8,128)(2,1)}, bf16[128,768]{1,0:T(8,128)(2,1)}, u32[]{:S(2)}, u32[]{:S(2)}) collective-permute-start(bf16[128,768]{1,0:T(8,128)(2,1)} %collective-permute-done.7), channel_id=1, source_target_pairs={{0,1},{1,0},{2,3},{3,2},{4,5},{5,4},{6,7},{7,6},{8,9},{9,8},{10,11... | collective-permute-start | bytes 589832 | tf_op jit(solution)/shard_map/ppermute | solution.py:61
  147.3 11.7 %collective-permute-start.10 = (bf16[256,768]{1,0:T(8,128)(2,1)S(1)}, bf16[256,768]{1,0:T(8,128)(2,1)S(1)}, u32[]{:S(2)}, u32[]{:S(2)}) collective-permute-start(bf16[256,768]{1,0:T(8,128)(2,1)S(1)} %get-tuple-element.73), channel_id=1, source_target_pairs={{0,2},{1,3},{2,0},{3,1},{4,6},{5,7},{6,4},{7,5},{8,10},{9,11},{10,... | collective-permute-start | bytes 1179656 | tf_op jit(solution)/shard_map/ppermute | solution.py:61
  147.6 14.4 %collective-permute-start.9 = (bf16[256,768]{1,0:T(8,128)(2,1)S(1)}, bf16[256,768]{1,0:T(8,128)(2,1)}, u32[]{:S(2)}, u32[]{:S(2)}) collective-permute-start(bf16[256,768]{1,0:T(8,128)(2,1)S(1)} %get-tuple-element.73), channel_id=1, source_target_pairs={{0,1},{1,0},{2,3},{3,2},{4,5},{5,4},{6,7},{7,6},{8,9},{9,8},{10,11... | collective-permute-start | bytes 1179656 | tf_op jit(solution)/shard_map/ppermute | solution.py:61
  231.5 25.0 %collective-permute-start.58 = (bf16[384,768]{1,0:T(8,128)(2,1)}, bf16[384,768]{1,0:T(8,128)(2,1)S(1)}, u32[]{:S(2)}, u32[]{:S(2)}) collective-permute-start(bf16[384,768]{1,0:T(8,128)(2,1)} %convolution_convert_fusion.10), channel_id=1, source_target_pairs={{0,1},{1,0},{2,3},{3,2},{4,5},{5,4},{6,7},{7,6},{8,9},{9,8},{10,11... | collective-permute-start | bytes 1769480 | tf_op jit(solution)/shard_map/ppermute | solution.py:61
  234.2 314.1 %collective-permute-start.74 = (bf16[384,3072]{1,0:T(8,128)(2,1)}, bf16[384,3072]{1,0:T(8,128)(2,1)}, u32[]{:S(2)}, u32[]{:S(2)}) collective-permute-start(bf16[384,3072]{1,0:T(8,128)(2,1)} %convolution_convert_fusion), channel_id=1, source_target_pairs={{0,1},{1,0},{2,3},{3,2},{4,5},{5,4},{6,7},{7,6},{8,9},{9,8},{10,11... | collective-permute-start | bytes 7077896 | tf_op jit(solution)/shard_map/ppermute | solution.py:61
  236.6 314.6 %collective-permute-start.90 = (bf16[1536,768]{1,0:T(8,128)(2,1)}, bf16[1536,768]{1,0:T(8,128)(2,1)}, u32[]{:S(2)}, u32[]{:S(2)}) collective-permute-start(bf16[1536,768]{1,0:T(8,128)(2,1)} %convolution_convert_fusion.4), channel_id=1, source_target_pairs={{0,1},{1,0},{2,3},{3,2},{4,5},{5,4},{6,7},{7,6},{8,9},{9,8},{10,11... | collective-permute-start | bytes 7077896 | tf_op jit(solution)/shard_map/ppermute | solution.py:61
  248.7 10.8 %collective-permute-start.34 = (bf16[384,768]{1,0:T(8,128)(2,1)S(1)}, bf16[384,768]{1,0:T(8,128)(2,1)S(1)}, u32[]{:S(2)}, u32[]{:S(2)}) collective-permute-start(bf16[384,768]{1,0:T(8,128)(2,1)S(1)} %convolution_convert_fusion.12), channel_id=1, source_target_pairs={{0,1},{1,0},{2,3},{3,2},{4,5},{5,4},{6,7},{7,6},{8,9},{9,8},{10,11... | collective-permute-start | bytes 1769480 | tf_op jit(solution)/shard_map/ppermute | solution.py:61
  256.5 12.0 %collective-permute-start.14 = (bf16[256,768]{1,0:T(8,128)(2,1)S(1)}, bf16[256,768]{1,0:T(8,128)(2,1)S(1)}, u32[]{:S(2)}, u32[]{:S(2)}) collective-permute-start(bf16[256,768]{1,0:T(8,128)(2,1)S(1)} %add_convert_fusion.40), channel_id=1, source_target_pairs={{0,2},{1,3},{2,0},{3,1},{4,6},{5,7},{6,4},{7,5},{8,10},{9,11},{10,... | collective-permute-start | bytes 1179656 | tf_op jit(solution)/shard_map/ppermute | solution.py:61
  259.5 108.9 %collective-permute-start.42 = (bf16[384,1536]{1,0:T(8,128)(2,1)}, bf16[384,1536]{1,0:T(8,128)(2,1)}, u32[]{:S(2)}, u32[]{:S(2)}) collective-permute-start(bf16[384,1536]{1,0:T(8,128)(2,1)} %convolution_convert_fusion.6), channel_id=1, source_target_pairs={{0,1},{1,0},{2,3},{3,2},{4,5},{5,4},{6,7},{7,6},{8,9},{9,8},{10,11... | collective-permute-start | bytes 3538952 | tf_op jit(solution)/shard_map/ppermute | solution.py:61
  260.9 65.8 %collective-permute-start.59 = (bf16[192,768]{1,0:T(8,128)(2,1)}, bf16[192,768]{1,0:T(8,128)(2,1)}, u32[]{:S(2)}, u32[]{:S(2)}) collective-permute-start(bf16[192,768]{1,0:T(8,128)(2,1)} %slice.364), channel_id=1, source_target_pairs={{0,2},{1,3},{2,0},{3,1},{4,6},{5,7},{6,4},{7,5},{8,10},{9,11},{10,... | collective-permute-start | bytes 884744 | tf_op jit(solution)/shard_map/ppermute | solution.py:61
  268.6 59.5 %collective-permute-start.35 = (bf16[192,768]{1,0:T(8,128)(2,1)}, bf16[192,768]{1,0:T(8,128)(2,1)}, u32[]{:S(2)}, u32[]{:S(2)}) collective-permute-start(bf16[192,768]{1,0:T(8,128)(2,1)} %slice.358), channel_id=1, source_target_pairs={{0,2},{1,3},{2,0},{3,1},{4,6},{5,7},{6,4},{7,5},{8,10},{9,11},{10,... | collective-permute-start | bytes 884744 | tf_op jit(solution)/shard_map/ppermute | solution.py:61
  326.7 54.5 %collective-permute-start.50 = (bf16[384,768]{1,0:T(8,128)(2,1)S(1)}, bf16[384,768]{1,0:T(8,128)(2,1)S(1)}, u32[]{:S(2)}, u32[]{:S(2)}) collective-permute-start(bf16[384,768]{1,0:T(8,128)(2,1)S(1)} %convolution_convert_fusion.11), channel_id=1, source_target_pairs={{0,1},{1,0},{2,3},{3,2},{4,5},{5,4},{6,7},{7,6},{8,9},{9,8},{10,11... | collective-permute-start | bytes 1769480 | tf_op jit(solution)/shard_map/ppermute | solution.py:61
  328.0 6.2 collective-permute-start.60
  368.3 14.1 %collective-permute-start.18 = (bf16[384,768]{1,0:T(8,128)(2,1)S(1)}, bf16[384,768]{1,0:T(8,128)(2,1)S(1)}, u32[]{:S(2)}, u32[]{:S(2)}) collective-permute-start(bf16[384,768]{1,0:T(8,128)(2,1)S(1)} %convolution_convert_fusion.13), channel_id=1, source_target_pairs={{0,1},{1,0},{2,3},{3,2},{4,5},{5,4},{6,7},{7,6},{8,9},{9,8},{10,11... | collective-permute-start | bytes 1769480 | tf_op jit(solution)/shard_map/ppermute | solution.py:61
  381.1 14.0 %collective-permute-start.15 = (bf16[256,768]{1,0:T(8,128)(2,1)S(1)}, bf16[256,768]{1,0:T(8,128)(2,1)S(1)}, u32[]{:S(2)}, u32[]{:S(2)}) collective-permute-start(bf16[256,768]{1,0:T(8,128)(2,1)S(1)} %get-tuple-element.106), channel_id=1, source_target_pairs={{0,1},{1,0},{2,3},{3,2},{4,5},{5,4},{6,7},{7,6},{8,9},{9,8},{10,11... | collective-permute-start | bytes 1179656 | tf_op jit(solution)/shard_map/ppermute | solution.py:61
  381.2 15.5 %collective-permute-start.17 = (bf16[256,768]{1,0:T(8,128)(2,1)S(1)}, bf16[256,768]{1,0:T(8,128)(2,1)S(1)}, u32[]{:S(2)}, u32[]{:S(2)}) collective-permute-start(bf16[256,768]{1,0:T(8,128)(2,1)S(1)} %add_convert_fusion.37), channel_id=1, source_target_pairs={{0,2},{1,3},{2,0},{3,1},{4,6},{5,7},{6,4},{7,5},{8,10},{9,11},{10,... | collective-permute-start | bytes 1179656 | tf_op jit(solution)/shard_map/ppermute | solution.py:61
  382.4 6.9 collective-permute-start.65
  395.1 203.0 %collective-permute-start.66 = (bf16[384,3072]{1,0:T(8,128)(2,1)}, bf16[384,3072]{1,0:T(8,128)(2,1)}, u32[]{:S(2)}, u32[]{:S(2)}) collective-permute-start(bf16[384,3072]{1,0:T(8,128)(2,1)} %convolution_convert_fusion.1), channel_id=1, source_target_pairs={{0,1},{1,0},{2,3},{3,2},{4,5},{5,4},{6,7},{7,6},{8,9},{9,8},{10,11... | collective-permute-start | bytes 7077896 | tf_op jit(solution)/shard_map/ppermute | solution.py:61
  395.1 66.4 %collective-permute-start.43 = (bf16[192,1536]{1,0:T(8,128)(2,1)}, bf16[192,1536]{1,0:T(8,128)(2,1)}, u32[]{:S(2)}, u32[]{:S(2)}) collective-permute-start(bf16[192,1536]{1,0:T(8,128)(2,1)} %slice.360), channel_id=1, source_target_pairs={{0,2},{1,3},{2,0},{3,1},{4,6},{5,7},{6,4},{7,5},{8,10},{9,11},{10,... | collective-permute-start | bytes 1769480 | tf_op jit(solution)/shard_map/ppermute | solution.py:61
  396.7 56.7 %collective-permute-start.51 = (bf16[192,768]{1,0:T(8,128)(2,1)}, bf16[192,768]{1,0:T(8,128)(2,1)}, u32[]{:S(2)}, u32[]{:S(2)}) collective-permute-start(bf16[192,768]{1,0:T(8,128)(2,1)} %slice.362), channel_id=1, source_target_pairs={{0,2},{1,3},{2,0},{3,1},{4,6},{5,7},{6,4},{7,5},{8,10},{9,11},{10,... | collective-permute-start | bytes 884744 | tf_op jit(solution)/shard_map/ppermute | solution.py:61
  453.4 8.0 %collective-permute-start.19 = (bf16[192,768]{1,0:T(8,128)(2,1)S(1)}, bf16[192,768]{1,0:T(8,128)(2,1)S(1)}, u32[]{:S(2)}, u32[]{:S(2)}) collective-permute-start(bf16[192,768]{1,0:T(8,128)(2,1)S(1)} %copy-done.114), channel_id=1, source_target_pairs={{0,2},{1,3},{2,0},{3,1},{4,6},{5,7},{6,4},{7,5},{8,10},{9,11},{10,... | collective-permute-start | bytes 884744 | tf_op jit(solution)/shard_map/ppermute | solution.py:61
  461.4 30.8 %collective-permute-start.26 = (bf16[384,1536]{1,0:T(8,128)(2,1)S(1)}, bf16[384,1536]{1,0:T(8,128)(2,1)S(1)}, u32[]{:S(2)}, u32[]{:S(2)}) collective-permute-start(bf16[384,1536]{1,0:T(8,128)(2,1)S(1)} %copy-done.178), channel_id=1, source_target_pairs={{0,1},{1,0},{2,3},{3,2},{4,5},{5,4},{6,7},{7,6},{8,9},{9,8},{10,11... | collective-permute-start | bytes 3538952 | tf_op jit(solution)/shard_map/ppermute | solution.py:61
  461.6 6.3 collective-permute-start.52
  492.2 109.8 %collective-permute-start.82 = (bf16[1536,768]{1,0:T(8,128)(2,1)S(1)}, bf16[1536,768]{1,0:T(8,128)(2,1)S(1)}, u32[]{:S(2)}, u32[]{:S(2)}) collective-permute-start(bf16[1536,768]{1,0:T(8,128)(2,1)S(1)} %copy-done.44), channel_id=1, source_target_pairs={{0,1},{1,0},{2,3},{3,2},{4,5},{5,4},{6,7},{7,6},{8,9},{9,8},{10,11... | collective-permute-start | bytes 7077896 | tf_op jit(solution)/shard_map/ppermute | solution.py:61
  511.6 8.3 %collective-permute-start.44 = (bf16[96,1536]{1,0:T(8,128)(2,1)S(1)}, bf16[96,1536]{1,0:T(8,128)(2,1)S(1)}, u32[]{:S(2)}, u32[]{:S(2)}) collective-permute-start(bf16[96,1536]{1,0:T(8,128)(2,1)S(1)} %constant_dynamic-slice_fusion.49), channel_id=1, source_target_pairs={{0,4},{4,0},{8,12},{12,8},{16,20},{20,16},{24,28},{28,24},{1,5},{5... | collective-permute-start | bytes 884744 | tf_op jit(solution)/shard_map/ppermute | solution.py:61
  546.6 16.3 %collective-permute-start.27 = (bf16[192,1536]{1,0:T(8,128)(2,1)S(1)}, bf16[192,1536]{1,0:T(8,128)(2,1)S(1)}, u32[]{:S(2)}, u32[]{:S(2)}) collective-permute-start(bf16[192,1536]{1,0:T(8,128)(2,1)S(1)} %slice.356), channel_id=1, source_target_pairs={{0,2},{1,3},{2,0},{3,1},{4,6},{5,7},{6,4},{7,5},{8,10},{9,11},{10,... | collective-permute-start | bytes 1769480 | tf_op jit(solution)/shard_map/ppermute | solution.py:61
  548.3 16.4 %collective-permute-start.48 = (bf16[48,1536]{1,0:T(8,128)(2,1)S(1)}, bf16[48,1536]{1,0:T(8,128)(2,1)S(1)}, u32[]{:S(2)}, u32[]{:S(2)}) collective-permute-start(bf16[48,1536]{1,0:T(8,128)(2,1)S(1)} %pad_maximum_fusion.16), channel_id=1, source_target_pairs={{0,8},{4,12},{8,0},{12,4},{16,24},{20,28},{24,16},{28,20},{1,9},{5... | collective-permute-start | bytes 442376 | tf_op jit(solution)/shard_map/ppermute | solution.py:61
  551.2 55.0 %collective-permute-start.75 = (bf16[192,3072]{1,0:T(8,128)(2,1)S(1)}, bf16[192,3072]{1,0:T(8,128)(2,1)S(1)}, u32[]{:S(2)}, u32[]{:S(2)}) collective-permute-start(bf16[192,3072]{1,0:T(8,128)(2,1)S(1)} %slice.368), channel_id=1, source_target_pairs={{0,2},{1,3},{2,0},{3,1},{4,6},{5,7},{6,4},{7,5},{8,10},{9,11},{10,... | collective-permute-start | bytes 3538952 | tf_op jit(solution)/shard_map/ppermute | solution.py:61
  562.9 50.6 %collective-permute-start.91 = (bf16[768,768]{1,0:T(8,128)(2,1)S(1)}, bf16[768,768]{1,0:T(8,128)(2,1)S(1)}, u32[]{:S(2)}, u32[]{:S(2)}) collective-permute-start(bf16[768,768]{1,0:T(8,128)(2,1)S(1)} %slice.372), channel_id=1, source_target_pairs={{0,2},{1,3},{2,0},{3,1},{4,6},{5,7},{6,4},{7,5},{8,10},{9,11},{10,... | collective-permute-start | bytes 3538952 | tf_op jit(solution)/shard_map/ppermute | solution.py:61
  564.7 6.8 collective-permute-start.28
  576.8 9.9 %collective-permute-start.49 = (bf16[96,1536]{1,0:T(8,128)(2,1)S(1)}, bf16[96,1536]{1,0:T(8,128)(2,1)S(1)}, u32[]{:S(2)}, u32[]{:S(2)}) collective-permute-start(bf16[96,1536]{1,0:T(8,128)(2,1)S(1)} %pad_maximum_fusion.6), channel_id=1, source_target_pairs={{0,4},{4,0},{8,12},{12,8},{16,20},{20,16},{24,28},{28,24},{1,5},{5... | collective-permute-start | bytes 884744 | tf_op jit(solution)/shard_map/ppermute | solution.py:61
  600.8 37.9 %collective-permute-start.67 = (bf16[192,3072]{1,0:T(8,128)(2,1)S(1)}, bf16[192,3072]{1,0:T(8,128)(2,1)S(1)}, u32[]{:S(2)}, u32[]{:S(2)}) collective-permute-start(bf16[192,3072]{1,0:T(8,128)(2,1)S(1)} %slice.366), channel_id=1, source_target_pairs={{0,2},{1,3},{2,0},{3,1},{4,6},{5,7},{6,4},{7,5},{8,10},{9,11},{10,... | collective-permute-start | bytes 3538952 | tf_op jit(solution)/shard_map/ppermute | solution.py:61
  603.0 48.8 %collective-permute-start.83 = (bf16[768,768]{1,0:T(8,128)(2,1)S(1)}, bf16[768,768]{1,0:T(8,128)(2,1)S(1)}, u32[]{:S(2)}, u32[]{:S(2)}) collective-permute-start(bf16[768,768]{1,0:T(8,128)(2,1)S(1)} %slice.370), channel_id=1, source_target_pairs={{0,2},{1,3},{2,0},{3,1},{4,6},{5,7},{6,4},{7,5},{8,10},{9,11},{10,... | collective-permute-start | bytes 3538952 | tf_op jit(solution)/shard_map/ppermute | solution.py:61
  604.0 11.4 %collective-permute-start.33 = (bf16[96,1536]{1,0:T(8,128)(2,1)S(1)}, bf16[96,1536]{1,0:T(8,128)(2,1)S(1)}, u32[]{:S(2)}, u32[]{:S(2)}) collective-permute-start(bf16[96,1536]{1,0:T(8,128)(2,1)S(1)} %pad_maximum_fusion.5), channel_id=1, source_target_pairs={{0,4},{4,0},{8,12},{12,8},{16,20},{20,16},{24,28},{28,24},{1,5},{5... | collective-permute-start | bytes 884744 | tf_op jit(solution)/shard_map/ppermute | solution.py:61
  606.7 11.2 %collective-permute-start.76 = (bf16[96,3072]{1,0:T(8,128)(2,1)S(1)}, bf16[96,3072]{1,0:T(8,128)(2,1)S(1)}, u32[]{:S(2)}, u32[]{:S(2)}) collective-permute-start(bf16[96,3072]{1,0:T(8,128)(2,1)S(1)} %constant_dynamic-slice_fusion.21), channel_id=1, source_target_pairs={{0,4},{4,0},{8,12},{12,8},{16,20},{20,16},{24,28},{28,24},{1,5},{5... | collective-permute-start | bytes 1769480 | tf_op jit(solution)/shard_map/ppermute | solution.py:61
  613.8 16.3 %collective-permute-start.92 = (bf16[384,768]{1,0:T(8,128)(2,1)S(1)}, bf16[384,768]{1,0:T(8,128)(2,1)S(1)}, u32[]{:S(2)}, u32[]{:S(2)}) collective-permute-start(bf16[384,768]{1,0:T(8,128)(2,1)S(1)} %constant_dynamic-slice_fusion.7), channel_id=1, source_target_pairs={{0,4},{4,0},{8,12},{12,8},{16,20},{20,16},{24,28},{28,24},{1,5},{5... | collective-permute-start | bytes 1769480 | tf_op jit(solution)/shard_map/ppermute | solution.py:61
  618.0 35.5 %collective-permute-start.77 = (bf16[48,3072]{1,0:T(8,128)(2,1)S(1)}, bf16[48,3072]{1,0:T(8,128)(2,1)S(1)}, u32[]{:S(2)}, u32[]{:S(2)}) collective-permute-start(bf16[48,3072]{1,0:T(8,128)(2,1)S(1)} %constant_dynamic-slice_fusion.20), channel_id=1, source_target_pairs={{0,8},{4,12},{8,0},{12,4},{16,24},{20,28},{24,16},{28,20},{1,9},{5... | collective-permute-start | bytes 884744 | tf_op jit(solution)/shard_map/ppermute | solution.py:61
  630.3 25.2 %collective-permute-start.93 = (bf16[192,768]{1,0:T(8,128)(2,1)S(1)}, bf16[192,768]{1,0:T(8,128)(2,1)S(1)}, u32[]{:S(2)}, u32[]{:S(2)}) collective-permute-start(bf16[192,768]{1,0:T(8,128)(2,1)S(1)} %constant_dynamic-slice_fusion.6), channel_id=1, source_target_pairs={{0,8},{4,12},{8,0},{12,4},{16,24},{20,28},{24,16},{28,20},{1,9},{5... | collective-permute-start | bytes 884744 | tf_op jit(solution)/shard_map/ppermute | solution.py:61
  639.2 34.3 %collective-permute-start.68 = (bf16[96,3072]{1,0:T(8,128)(2,1)S(1)}, bf16[96,3072]{1,0:T(8,128)(2,1)S(1)}, u32[]{:S(2)}, u32[]{:S(2)}) collective-permute-start(bf16[96,3072]{1,0:T(8,128)(2,1)S(1)} %constant_dynamic-slice_fusion.28), channel_id=1, source_target_pairs={{0,4},{4,0},{8,12},{12,8},{16,20},{20,16},{24,28},{28,24},{1,5},{5... | collective-permute-start | bytes 1769480 | tf_op jit(solution)/shard_map/ppermute | solution.py:61
  652.1 21.8 %collective-permute-start.84 = (bf16[384,768]{1,0:T(8,128)(2,1)S(1)}, bf16[384,768]{1,0:T(8,128)(2,1)S(1)}, u32[]{:S(2)}, u32[]{:S(2)}) collective-permute-start(bf16[384,768]{1,0:T(8,128)(2,1)S(1)} %constant_dynamic-slice_fusion.14), channel_id=1, source_target_pairs={{0,4},{4,0},{8,12},{12,8},{16,20},{20,16},{24,28},{28,24},{1,5},{5... | collective-permute-start | bytes 1769480 | tf_op jit(solution)/shard_map/ppermute | solution.py:61
  653.6 7.1 collective-permute-start.78
  655.6 8.2 %collective-permute-start.94 = (bf16[96,768]{1,0:T(8,128)(2,1)S(1)}, bf16[96,768]{1,0:T(8,128)(2,1)S(1)}, u32[]{:S(2)}, u32[]{:S(2)}) collective-permute-start(bf16[96,768]{1,0:T(8,128)(2,1)S(1)} %constant_dynamic-slice_fusion.5), channel_id=1, source_target_pairs={{0,16},{4,20},{8,24},{12,28},{16,0},{20,4},{24,8},{28,12},{1,17},{... | collective-permute-start | bytes 442376 | tf_op jit(solution)/shard_map/ppermute | solution.py:61
  660.7 6.8 collective-permute-start.79
  663.8 7.7 %collective-permute-start.95 = (bf16[96,768]{1,0:T(8,128)(2,1)S(1)}, bf16[96,768]{1,0:T(8,128)(2,1)S(1)}, u32[]{:S(2)}, u32[]{:S(2)}) collective-permute-start(bf16[96,768]{1,0:T(8,128)(2,1)S(1)} %add_convert_fusion.52), channel_id=1, source_target_pairs={{0,16},{4,20},{8,24},{12,28},{16,0},{20,4},{24,8},{28,12},{1,17},{... | collective-permute-start | bytes 442376 | tf_op jit(solution)/shard_map/ppermute | solution.py:61
  667.6 10.7 %collective-permute-start.80 = (bf16[48,3072]{1,0:T(8,128)(2,1)S(1)}, bf16[48,3072]{1,0:T(8,128)(2,1)S(1)}, u32[]{:S(2)}, u32[]{:S(2)}) collective-permute-start(bf16[48,3072]{1,0:T(8,128)(2,1)S(1)} %pad_maximum_fusion.8), channel_id=1, source_target_pairs={{0,8},{4,12},{8,0},{12,4},{16,24},{20,28},{24,16},{28,20},{1,9},{5... | collective-permute-start | bytes 884744 | tf_op jit(solution)/shard_map/ppermute | solution.py:61
  671.6 13.4 %collective-permute-start.96 = (bf16[192,768]{1,0:T(8,128)(2,1)S(1)}, bf16[192,768]{1,0:T(8,128)(2,1)S(1)}, u32[]{:S(2)}, u32[]{:S(2)}) collective-permute-start(bf16[192,768]{1,0:T(8,128)(2,1)S(1)} %pad_maximum_fusion.10), channel_id=1, source_target_pairs={{0,8},{4,12},{8,0},{12,4},{16,24},{20,28},{24,16},{28,20},{1,9},{5... | collective-permute-start | bytes 884744 | tf_op jit(solution)/shard_map/ppermute | solution.py:61
  673.7 15.1 %collective-permute-start.69 = (bf16[48,3072]{1,0:T(8,128)(2,1)S(1)}, bf16[48,3072]{1,0:T(8,128)(2,1)S(1)}, u32[]{:S(2)}, u32[]{:S(2)}) collective-permute-start(bf16[48,3072]{1,0:T(8,128)(2,1)S(1)} %constant_dynamic-slice_fusion.27), channel_id=1, source_target_pairs={{0,8},{4,12},{8,0},{12,4},{16,24},{20,28},{24,16},{28,20},{1,9},{5... | collective-permute-start | bytes 884744 | tf_op jit(solution)/shard_map/ppermute | solution.py:61
  674.1 21.2 %collective-permute-start.85 = (bf16[192,768]{1,0:T(8,128)(2,1)S(1)}, bf16[192,768]{1,0:T(8,128)(2,1)S(1)}, u32[]{:S(2)}, u32[]{:S(2)}) collective-permute-start(bf16[192,768]{1,0:T(8,128)(2,1)S(1)} %constant_dynamic-slice_fusion.13), channel_id=1, source_target_pairs={{0,8},{4,12},{8,0},{12,4},{16,24},{20,28},{24,16},{28,20},{1,9},{5... | collective-permute-start | bytes 884744 | tf_op jit(solution)/shard_map/ppermute | solution.py:61
  678.4 32.6 %collective-permute-start.81 = (bf16[96,3072]{1,0:T(8,128)(2,1)S(1)}, bf16[96,3072]{1,0:T(8,128)(2,1)S(1)}, u32[]{:S(2)}, u32[]{:S(2)}) collective-permute-start(bf16[96,3072]{1,0:T(8,128)(2,1)S(1)} %pad_maximum_fusion.1), channel_id=1, source_target_pairs={{0,4},{4,0},{8,12},{12,8},{16,20},{20,16},{24,28},{28,24},{1,5},{5... | collective-permute-start | bytes 1769480 | tf_op jit(solution)/shard_map/ppermute | solution.py:61
  685.1 30.1 %collective-permute-start.97 = (bf16[384,768]{1,0:T(8,128)(2,1)S(1)}, bf16[384,768]{1,0:T(8,128)(2,1)S(1)}, u32[]{:S(2)}, u32[]{:S(2)}) collective-permute-start(bf16[384,768]{1,0:T(8,128)(2,1)S(1)} %pad_maximum_fusion.3), channel_id=1, source_target_pairs={{0,4},{4,0},{8,12},{12,8},{16,20},{20,16},{24,28},{28,24},{1,5},{5... | collective-permute-start | bytes 1769480 | tf_op jit(solution)/shard_map/ppermute | solution.py:61
  688.8 9.7 %collective-permute-start.70 = (bf16[24,3072]{1,0:T(8,128)(2,1)S(1)}, bf16[24,3072]{1,0:T(8,128)(2,1)S(1)}, u32[]{:S(2)}, u32[]{:S(2)}) collective-permute-start(bf16[24,3072]{1,0:T(8,128)(2,1)S(1)} %constant_dynamic-slice_fusion.26), channel_id=1, source_target_pairs={{0,16},{4,20},{8,24},{12,28},{16,0},{20,4},{24,8},{28,12},{1,17},{... | collective-permute-start | bytes 442376 | tf_op jit(solution)/shard_map/ppermute | solution.py:61
  695.5 7.1 collective-permute-start.86
  698.6 7.1 collective-permute-start.71
  702.6 8.3 %collective-permute-start.87 = (bf16[96,768]{1,0:T(8,128)(2,1)S(1)}, bf16[96,768]{1,0:T(8,128)(2,1)S(1)}, u32[]{:S(2)}, u32[]{:S(2)}) collective-permute-start(bf16[96,768]{1,0:T(8,128)(2,1)S(1)} %add_convert_fusion.53), channel_id=1, source_target_pairs={{0,16},{4,20},{8,24},{12,28},{16,0},{20,4},{24,8},{28,12},{1,17},{... | collective-permute-start | bytes 442376 | tf_op jit(solution)/shard_map/ppermute | solution.py:61
  705.7 8.1 %collective-permute-start.72 = (bf16[48,3072]{1,0:T(8,128)(2,1)S(1)}, bf16[48,3072]{1,0:T(8,128)(2,1)S(1)}, u32[]{:S(2)}, u32[]{:S(2)}) collective-permute-start(bf16[48,3072]{1,0:T(8,128)(2,1)S(1)} %pad_maximum_fusion.7), channel_id=1, source_target_pairs={{0,8},{4,12},{8,0},{12,4},{16,24},{20,28},{24,16},{28,20},{1,9},{5... | collective-permute-start | bytes 884744 | tf_op jit(solution)/shard_map/ppermute | solution.py:61
  711.0 6.8 collective-permute-start.88
  714.0 10.8 %collective-permute-start.73 = (bf16[96,3072]{1,0:T(8,128)(2,1)S(1)}, bf16[96,3072]{1,0:T(8,128)(2,1)S(1)}, u32[]{:S(2)}, u32[]{:S(2)}) collective-permute-start(bf16[96,3072]{1,0:T(8,128)(2,1)S(1)} %pad_maximum_fusion), channel_id=1, source_target_pairs={{0,4},{4,0},{8,12},{12,8},{16,20},{20,16},{24,28},{28,24},{1,5},{5... | collective-permute-start | bytes 1769480 | tf_op jit(solution)/shard_map/ppermute | solution.py:61
  717.9 13.1 %collective-permute-start.89 = (bf16[384,768]{1,0:T(8,128)(2,1)S(1)}, bf16[384,768]{1,0:T(8,128)(2,1)S(1)}, u32[]{:S(2)}, u32[]{:S(2)}) collective-permute-start(bf16[384,768]{1,0:T(8,128)(2,1)S(1)} %pad_maximum_fusion.2), channel_id=1, source_target_pairs={{0,4},{4,0},{8,12},{12,8},{16,20},{20,16},{24,28},{28,24},{1,5},{5... | collective-permute-start | bytes 1769480 | tf_op jit(solution)/shard_map/ppermute | solution.py:61
  (254 other events, 2415.5 us)
